TPU v7x, 32 devices: a whole 2x2x4 slice. The times are simulated.
32 devices in a mesh: groups: 2 (over y), expert: 4 (over z), dp: 2 (over x), sub: 2 (over core).
Axes of the slice: x: 2, y: 2, z: 4, core: 2. Of those that a mesh axis runs over, the one named last changes fastest.
Arguments:
- tokens: bfloat16 [4096, 2048], P(('groups', 'expert', 'dp', 'sub')), parts along dimension 0, may hold values from -6 to 6
- cotangent: bfloat16 [4096, 2048], P(('groups', 'expert', 'dp', 'sub')), parts along dimension 0, may hold values from -6 to 6
- gate_prob: float32 [4096], P(('groups', 'expert', 'dp', 'sub')), parts along dimension 0, may hold values from 0.25 to 1
- target_device: int32 [4096], P(('groups', 'expert', 'dp', 'sub')), parts along dimension 0, may hold values from 0 to 3, as said below
- use_copy: int32 [4096], P(('groups', 'expert', 'dp', 'sub')), parts along dimension 0, may hold values from 0 to 1
- hot_experts: int32 [4], P('groups'), parts along dimension 0, may hold values from 0 to 3, as said below
- copy_slot: int32 [8], P('groups'), parts along dimension 0, may hold values from 0 to 1, as said below
- gate_weight: bfloat16 [4, 2048, 768], P('expert', None, 'sub'), may hold values from -0.125 to 0.125
- up_weight: bfloat16 [4, 2048, 768], P('expert', None, 'sub'), may hold values from -0.125 to 0.125
- down_weight: bfloat16 [4, 768, 2048], P('expert', 'sub'), may hold values from -0.21875 to 0.21875
Outputs:
- layer_out: bfloat16 [4096, 2048], P(('groups', 'expert', 'dp', 'sub')), parts along dimension 0
- token_grad: bfloat16 [4096, 2048], P(('groups', 'expert', 'dp', 'sub')), parts along dimension 0
- prob_grad: float32 [4096], P(('groups', 'expert', 'dp', 'sub')), parts along dimension 0
- gate_weight_grad: float32 [8, 2048, 768], P(('groups', 'expert'), 'dp', 'sub'), parts along dimension 0
- up_weight_grad: float32 [8, 2048, 768], P(('groups', 'expert'), 'dp', 'sub'), parts along dimension 0
- down_weight_grad: float32 [8, 768, 2048], P(('groups', 'expert'), 'sub', 'dp'), parts along dimension 0
There are 2 independent parts, one for each index of `groups`. A program takes and returns all parts, laid end to end along the dimension named above; an argument that names none is the same for every part. Nothing has to cross between parts.
Inputs may be any that keep to these rules, and one draw needn't show every extreme that they name: Among the 128 rows of one device, at most 24 have any one pair of target_device and use_copy; in every such block some pair has exactly 24 rows, and the pair (hot_experts[0], 0) has exactly 24 rows in every block. `hot_experts`: distinct experts. copy_slot[hot_experts[0]] = 1 and copy_slot[hot_experts[1]] = 0: a hot expert's own device holds the other one's copy.
All inputs are finite; a program needn't handle non-finite values.
Results may differ from a plain program's by a relative error of at most 0.0095.
Values may be sent and summed in bfloat16 or wider, within the bound.
A program may use at most 128 MiB of HBM per device.

v0:
```python
import jax
import jax.numpy as jnp
from jax import lax
from jax.sharding import PartitionSpec as P

NHOT = 2


def broadcast(value, axis, source):
    kept = jnp.where(lax.axis_index(axis) == source, value, 0).astype(value.dtype)
    return lax.psum(kept, axis)


def expert_pass(rows_in, scaled_rows, gate_weight, up_weight, down_weight):
    across = (((1,), (1,)), ((), ()))
    contract = (((0,), (0,)), ((), ()))
    gate_in = jnp.dot(rows_in, gate_weight, preferred_element_type=jnp.float32)
    up_in = jnp.dot(rows_in, up_weight, preferred_element_type=jnp.float32)
    sigmoid_gate = jax.nn.sigmoid(gate_in)
    active = gate_in * sigmoid_gate
    hidden = (active * up_in).astype(jnp.bfloat16)
    out_part = jnp.dot(hidden, down_weight, preferred_element_type=jnp.float32)
    hidden_grad = lax.dot_general(
        scaled_rows, down_weight, across, preferred_element_type=jnp.float32
    )
    gate_grad = (
        hidden_grad * up_in * sigmoid_gate * (1.0 + gate_in * (1.0 - sigmoid_gate))
    ).astype(jnp.bfloat16)
    up_grad = (hidden_grad * active).astype(jnp.bfloat16)
    row_grad = lax.dot_general(gate_grad, gate_weight, across, preferred_element_type=jnp.float32)
    row_grad = row_grad + lax.dot_general(
        up_grad, up_weight, across, preferred_element_type=jnp.float32
    )
    part_gate = lax.dot_general(rows_in, gate_grad, contract, preferred_element_type=jnp.float32)
    part_up = lax.dot_general(rows_in, up_grad, contract, preferred_element_type=jnp.float32)
    part_down = lax.dot_general(hidden, scaled_rows, contract, preferred_element_type=jnp.float32)
    return (out_part, row_grad, (part_gate, part_up, part_down))


def on_device(
    tokens,
    cotangent,
    gate_prob,
    target_device,
    use_copy,
    hot_experts,
    copy_slot,
    gate_weight,
    up_weight,
    down_weight,
):
    row_count = tokens.shape[0]
    model_width = tokens.shape[1]
    experts = lax.axis_size("expert")
    halves = lax.axis_size("sub")
    capacity = row_count * 3 // (experts * 4)
    classes = 2 * experts
    myself = lax.axis_index("expert")
    slot_class = target_device * 2 + use_copy
    member = (slot_class[:, None] == jnp.arange(classes, dtype=jnp.int32)[None, :]).astype(
        jnp.int32
    )
    earlier = jnp.cumsum(member, axis=0) - member
    slot_rank = jnp.sum(earlier * member, axis=1)
    slot_index = slot_class * capacity + slot_rank
    placing = (
        jnp.arange(classes * capacity, dtype=jnp.int32)[:, None] == slot_index[None, :]
    ).astype(jnp.bfloat16)
    scaled = (gate_prob[:, None] * cotangent.astype(jnp.float32)).astype(jnp.bfloat16)
    send_rows = jnp.dot(placing, tokens, preferred_element_type=jnp.float32).astype(jnp.bfloat16)
    send_rows = send_rows.reshape(experts, 1, 2 * capacity, model_width)
    send_scaled = jnp.dot(placing, scaled, preferred_element_type=jnp.float32).astype(jnp.bfloat16)
    send_scaled = send_scaled.reshape(experts, 1, 2 * capacity, model_width)
    both_rows = jnp.broadcast_to(send_rows, (experts, halves, 2 * capacity, model_width))
    both_scaled = jnp.broadcast_to(send_scaled, (experts, halves, 2 * capacity, model_width))
    got_rows, got_scaled = (
        lax.all_to_all(
            lax.all_to_all(both_rows, "expert", split_axis=0, concat_axis=0, tiled=True),
            "sub",
            split_axis=1,
            concat_axis=1,
            tiled=True,
        ),
        lax.all_to_all(
            lax.all_to_all(both_scaled, "expert", split_axis=0, concat_axis=0, tiled=True),
            "sub",
            split_axis=1,
            concat_axis=1,
            tiled=True,
        ),
    )
    hosted_slot = jnp.sum(jnp.where(jnp.arange(experts, dtype=jnp.int32) == myself, copy_slot, 0))
    own_weights = (gate_weight[0], up_weight[0], down_weight[0])
    share_width = model_width // lax.axis_size("dp")
    first_row = lax.axis_index("dp") * share_width
    own_shares = (
        lax.dynamic_slice_in_dim(own_weights[0], first_row, share_width, 0),
        lax.dynamic_slice_in_dim(own_weights[1], first_row, share_width, 0),
        lax.dynamic_slice_in_dim(own_weights[2], first_row, share_width, 1),
    )
    copy_shares = own_shares
    for hot_slot in range(NHOT):
        fetched = (
            broadcast(own_shares[0], "expert", hot_experts[hot_slot]),
            broadcast(own_shares[1], "expert", hot_experts[hot_slot]),
            broadcast(own_shares[2], "expert", hot_experts[hot_slot]),
        )
        copy_shares = jax.tree.map(
            lambda kept_value, new_value: jnp.where(hosted_slot == hot_slot, new_value, kept_value),
            copy_shares,
            fetched,
        )
    copy_weights = (
        lax.all_gather(copy_shares[0], "dp", axis=0, tiled=True),
        lax.all_gather(copy_shares[1], "dp", axis=0, tiled=True),
        lax.all_gather(copy_shares[2], "dp", axis=1, tiled=True),
    )
    grouped = got_rows.reshape(experts, halves, 2, capacity, model_width)
    grouped_scaled = got_scaled.reshape(experts, halves, 2, capacity, model_width)
    own_out, own_grad, own_parts = expert_pass(
        grouped[:, :, 0].reshape(-1, model_width),
        grouped_scaled[:, :, 0].reshape(-1, model_width),
        own_weights[0],
        own_weights[1],
        own_weights[2],
    )
    copy_out, copy_grad, copy_parts = expert_pass(
        grouped[:, :, 1].reshape(-1, model_width),
        grouped_scaled[:, :, 1].reshape(-1, model_width),
        copy_weights[0],
        copy_weights[1],
        copy_weights[2],
    )
    shape_back = (experts, halves, 1, capacity, model_width)
    out_all = jnp.concatenate((own_out.reshape(shape_back), copy_out.reshape(shape_back)), axis=2)
    out_all = out_all.reshape(experts, halves, 2 * capacity, model_width)
    grad_all = jnp.concatenate(
        (own_grad.reshape(shape_back), copy_grad.reshape(shape_back)), axis=2
    )
    grad_all = grad_all.reshape(experts, halves, 2 * capacity, model_width)
    back_out, back_grad = (
        lax.all_to_all(
            lax.all_to_all(
                out_all.astype(jnp.bfloat16), "expert", split_axis=0, concat_axis=0, tiled=True
            ),
            "sub",
            split_axis=1,
            concat_axis=1,
            tiled=True,
        ).astype(out_all.dtype),
        lax.all_to_all(
            lax.all_to_all(
                grad_all.astype(jnp.bfloat16), "expert", split_axis=0, concat_axis=0, tiled=True
            ),
            "sub",
            split_axis=1,
            concat_axis=1,
            tiled=True,
        ).astype(grad_all.dtype),
    )
    expert_out = jnp.sum(back_out, axis=1).astype(jnp.bfloat16)
    expert_grad = jnp.sum(back_grad, axis=1).astype(jnp.bfloat16)
    contract = (((0,), (0,)), ((), ()))
    out_rows = lax.dot_general(
        placing,
        expert_out.reshape(classes * capacity, model_width),
        contract,
        preferred_element_type=jnp.float32,
    )
    grad_rows = lax.dot_general(
        placing,
        expert_grad.reshape(classes * capacity, model_width),
        contract,
        preferred_element_type=jnp.float32,
    )
    layer_out = (gate_prob[:, None] * out_rows).astype(jnp.bfloat16)
    prob_grad = jnp.sum(cotangent.astype(jnp.float32) * out_rows, axis=1)
    token_grad = grad_rows.astype(jnp.bfloat16)
    summed = (
        lax.psum_scatter(
            own_parts[0].astype(jnp.bfloat16), "dp", scatter_dimension=0, tiled=True
        ).astype(jnp.float32),
        lax.psum_scatter(
            own_parts[1].astype(jnp.bfloat16), "dp", scatter_dimension=0, tiled=True
        ).astype(jnp.float32),
        lax.psum_scatter(
            own_parts[2].astype(jnp.bfloat16), "dp", scatter_dimension=1, tiled=True
        ).astype(jnp.float32),
        lax.psum_scatter(
            copy_parts[0].astype(jnp.bfloat16), "dp", scatter_dimension=0, tiled=True
        ).astype(jnp.float32),
        lax.psum_scatter(
            copy_parts[1].astype(jnp.bfloat16), "dp", scatter_dimension=0, tiled=True
        ).astype(jnp.float32),
        lax.psum_scatter(
            copy_parts[2].astype(jnp.bfloat16), "dp", scatter_dimension=1, tiled=True
        ).astype(jnp.float32),
    )
    first_slots = [jnp.where(hosted_slot == 0, piece_sum, 0.0) for piece_sum in summed[3:]]
    second_slots = [jnp.where(hosted_slot == 1, piece_sum, 0.0) for piece_sum in summed[3:]]
    totals = (
        lax.psum(first_slots[0].astype(jnp.bfloat16), "expert").astype(jnp.float32),
        lax.psum(first_slots[1].astype(jnp.bfloat16), "expert").astype(jnp.float32),
        lax.psum(first_slots[2].astype(jnp.bfloat16), "expert").astype(jnp.float32),
        lax.psum(second_slots[0].astype(jnp.bfloat16), "expert").astype(jnp.float32),
        lax.psum(second_slots[1].astype(jnp.bfloat16), "expert").astype(jnp.float32),
        lax.psum(second_slots[2].astype(jnp.bfloat16), "expert").astype(jnp.float32),
    )
    finals = [summed[0], summed[1], summed[2]]
    for hot_slot in range(NHOT):
        is_home = hot_experts[hot_slot] == myself
        for position in range(3):
            finals[position] = finals[position] + jnp.where(
                is_home, totals[3 * hot_slot + position], 0.0
            )
    return (layer_out, token_grad, prob_grad, finals[0][None], finals[1][None], finals[2][None])


def solution(mesh):
    placed = (
        P(("groups", "expert", "dp", "sub"), None),
        P(("groups", "expert", "dp", "sub"), None),
        P(("groups", "expert", "dp", "sub")),
        P(("groups", "expert", "dp", "sub")),
        P(("groups", "expert", "dp", "sub")),
        P("groups"),
        P("groups"),
        P("expert", None, "sub"),
        P("expert", None, "sub"),
        P("expert", "sub", None),
    )
    return jax.shard_map(
        on_device,
        mesh=mesh,
        in_specs=placed,
        out_specs=(
            P(("groups", "expert", "dp", "sub"), None),
            P(("groups", "expert", "dp", "sub"), None),
            P(("groups", "expert", "dp", "sub")),
            P(("groups", "expert"), "dp", "sub"),
            P(("groups", "expert"), "dp", "sub"),
            P(("groups", "expert"), "sub", "dp"),
        ),
        check_vma=False,
    )
```

profile of v0, /device:TPU:0, one launch (start us, length us, event | category | flops | bytes accessed | tf_op | source)
XLA Modules:
  0.0 722.6 jit_solution(4706204567664985885)
XLA Ops:
  12.7 3.1 bitcast_select_fusion.4
  18.6 6.4 all-to-all-start
  27.0 198.7 %all-reduce.7.cloned.1.call-done = (bf16[1024,384]{1,0:T(8,128)(2,1)}, bf16[1024,384]{1,0:T(8,128)(2,1)}, bf16[1024,384]{1,0:T(8,128)(2,1)}, bf16[1024,384]{1,0:...) async-done(((bf16[1024,384]{1,0:T(8,128)(2,1)}, bf16[1024,384]{1,0:T(8,128)(2,1)}, bf16[1024,384]{1,0:T(8,128)(2,1)}, bf16[1024,384]{1,0:T(8,128)(2,1)}, ...) | async-done | bytes 4718608 | tf_op jit(solution)/shard_map/psum | solution.py:11
  229.9 4.5 all-to-all-start.4
  239.6 32.1 %all-to-all-done.4 = bf16[4,2,48,2048]{3,2,1,0:T(8,128)(2,1)} async-done(((bf16[4,2,48,2048]{3,2,1,0:T(8,128)(2,1)}), bf16[4,2,48,2048]{3,2,1,0:T(8,128)(2,1)}, u32[]{:S(2)}, u32[]{:S(2)}) %all-to-all-start.4) | async-done | bytes 1572896 | tf_op jit(solution)/shard_map/all_to_all | solution.py:85
  271.7 3.7 all-to-all-start.1
  278.1 4.6 all-to-all-start.5
  298.4 17.6 %all-gather.8.cloned.1.call-done = bf16[384,2048]{1,0:T(8,128)(2,1)} async-done(((bf16[384,1024]{1,0:T(8,128)(2,1)}), bf16[384,2048]{1,0:T(8,128)(2,1)}) %all-gather.8.cloned.1.call-update) | async-done | bytes 1572880 | tf_op jit(solution)/shard_map/all_gather | solution.py:116
  316.0 3.2 multiply_convert_fusion.1
  334.4 12.9 %reduce-scatter.9.cloned.1.call-done = bf16[1024,384]{1,0:T(8,128)(2,1)} async-done(((bf16[2048,384]{1,0:T(8,128)(2,1)}), bf16[1024,384]{1,0:T(8,128)(2,1)}) %reduce-scatter.9.cloned.1.call-update) | async-done | bytes 786448 | tf_op jit(solution)/shard_map/reduce_scatter | solution.py:189
  349.9 26.2 %reduce-scatter.13.cloned.1.call-done = bf16[1024,384]{1,0:T(8,128)(2,1)} async-done(((bf16[2048,384]{1,0:T(8,128)(2,1)}), bf16[1024,384]{1,0:T(8,128)(2,1)}) %reduce-scatter.13.cloned.1.call-update) | async-done | bytes 786448 | tf_op jit(solution)/shard_map/reduce_scatter | solution.py:192
  378.7 26.4 %reduce-scatter.17.cloned.1.call-done = bf16[384,1024]{1,0:T(8,128)(2,1)} async-done(((bf16[384,2048]{1,0:T(8,128)(2,1)}), bf16[384,1024]{1,0:T(8,128)(2,1)}) %reduce-scatter.17.cloned.1.call-update) | async-done | bytes 786448 | tf_op jit(solution)/shard_map/reduce_scatter | solution.py:195
  418.0 4.7 all-to-all-start.2
  429.4 55.1 %all-to-all-done.2 = bf16[4,2,48,2048]{3,2,1,0:T(8,128)(2,1)S(1)} async-done(((bf16[4,2,48,2048]{3,2,1,0:T(8,128)(2,1)}), bf16[4,2,48,2048]{3,2,1,0:T(8,128)(2,1)S(1)}, u32[]{:S(2)}, u32[]{:S(2)}) %all-to-all-start.2) | async-done | bytes 1572896 | tf_op jit(solution)/shard_map/all_to_all | solution.py:143
  484.5 7.6 %all-to-all-start.6 = ((bf16[4,2,48,2048]{3,2,1,0:T(8,128)(2,1)}), bf16[4,2,48,2048]{3,2,1,0:T(8,128)(2,1)S(1)}, u32[]{:S(2)}, u32[]{:S(2)}) async-start(bf16[4,2,48,2048]{3,2,1,0:T(8,128)(2,1)} %bitcast.110), calls=%async_computation.6 | async-start | bytes 3145728 | tf_op jit(solution)/shard_map/all_to_all | solution.py:152
  492.0 2.9 convolution_convert_fusion.1
  497.5 62.2 %all-to-all-done.6 = bf16[4,2,48,2048]{3,2,1,0:T(8,128)(2,1)S(1)} async-done(((bf16[4,2,48,2048]{3,2,1,0:T(8,128)(2,1)}), bf16[4,2,48,2048]{3,2,1,0:T(8,128)(2,1)S(1)}, u32[]{:S(2)}, u32[]{:S(2)}) %all-to-all-start.6) | async-done | bytes 1572896 | tf_op jit(solution)/shard_map/all_to_all | solution.py:152
  559.7 3.7 all-to-all-start.3
  565.9 3.7 all-to-all-start.7
  576.5 81.3 %all-reduce.5.cloned.1.call-done = (bf16[1024,384]{1,0:T(8,128)(2,1)}, bf16[1024,384]{1,0:T(8,128)(2,1)}, bf16[1024,384]{1,0:T(8,128)(2,1)}, bf16[1024,384]{1,0:...) async-done(((bf16[1024,384]{1,0:T(8,128)(2,1)}, bf16[1024,384]{1,0:T(8,128)(2,1)}, bf16[1024,384]{1,0:T(8,128)(2,1)}, bf16[1024,384]{1,0:T(8,128)(2,1)}, ...) | async-done | bytes 4718608 | tf_op jit(solution)/shard_map/psum | solution.py:205
  657.8 3.2 add_bitcast_fusion.2
  660.9 23.9 %reduce-scatter.11.cloned.1.call-done = bf16[1024,384]{1,0:T(8,128)(2,1)} async-done(((bf16[2048,384]{1,0:T(8,128)(2,1)}), bf16[1024,384]{1,0:T(8,128)(2,1)}) %reduce-scatter.11.cloned.1.call-update) | async-done | bytes 786448 | tf_op jit(solution)/shard_map/reduce_scatter | solution.py:183
  684.8 3.0 add_bitcast_fusion.1
  687.8 25.5 %reduce-scatter.15.cloned.1.call-done = bf16[384,1024]{1,0:T(8,128)(2,1)} async-done(((bf16[384,2048]{1,0:T(8,128)(2,1)}), bf16[384,1024]{1,0:T(8,128)(2,1)}) %reduce-scatter.15.cloned.1.call-update) | async-done | bytes 786448 | tf_op jit(solution)/shard_map/reduce_scatter | solution.py:186
  (142 shorter events, 88.3 us)
Async XLA Ops:
  7.2 9.7 %copy-start = (bf16[128,2048]{1,0:T(8,128)(2,1)S(1)}, bf16[128,2048]{1,0:T(8,128)(2,1)}, u32[]{:S(2)}) copy-start(bf16[128,2048]{1,0:T(8,128)(2,1)} %param.10) | copy-start | bytes 1572868
  7.2 218.5 %all-reduce.7.cloned.1.call-start = ((), (), s32[]{:S(2)}) async-start(), calls=%async_computation.24 | async-start | bytes 9437184 | tf_op jit(solution)/shard_map/psum | solution.py:11
  18.6 210.0 %all-to-all-start = ((bf16[4,2,48,2048]{3,2,1,0:T(8,128)(2,1)}), bf16[4,2,48,2048]{3,2,1,0:T(8,128)(2,1)}, u32[]{:S(2)}, u32[]{:S(2)}) async-start(bf16[4,2,48,2048]{3,2,1,0:T(8,128)(2,1)} %broadcast_in_dim.64), calls=%async_computation | async-start | bytes 3145728 | tf_op jit(solution)/shard_map/all_to_all | solution.py:78
  25.0 267.9 %all-gather.4.cloned.1.call-start = ((), (), s32[]{:S(2)}) async-start(), calls=%async_computation.14 | async-start | bytes 2359296 | tf_op jit(solution)/shard_map/all_gather | solution.py:114
  229.9 41.8 %all-to-all-start.4 = ((bf16[4,2,48,2048]{3,2,1,0:T(8,128)(2,1)}), bf16[4,2,48,2048]{3,2,1,0:T(8,128)(2,1)}, u32[]{:S(2)}, u32[]{:S(2)}) async-start(bf16[4,2,48,2048]{3,2,1,0:T(8,128)(2,1)} %broadcast_in_dim.69), calls=%async_computation.4 | async-start | bytes 3145728 | tf_op jit(solution)/shard_map/all_to_all | solution.py:85
  234.5 61.2 %all-gather.6.cloned.1.call-start = ((), (), s32[]{:S(2)}) async-start(), calls=%async_computation.15 | async-start | bytes 2359296 | tf_op jit(solution)/shard_map/all_gather | solution.py:115
  271.7 6.4 all-to-all-start.1
  278.1 7.2 %all-to-all-start.5 = ((bf16[4,2,48,2048]{3,2,0,1:T(8,128)(2,1)}), bf16[4,2,48,2048]{3,2,0,1:T(8,128)(2,1)}, u32[]{:S(2)}, u32[]{:S(2)}) async-start(bf16[4,2,48,2048]{3,2,0,1:T(8,128)(2,1)} %copy.40), calls=%async_computation.5 | async-start | bytes 3145728 | tf_op jit(solution)/shard_map/all_to_all | solution.py:84
  282.8 33.2 %all-gather.8.cloned.1.call-start = ((), (), s32[]{:S(2)}) async-start(), calls=%async_computation.16 | async-start | bytes 2359296 | tf_op jit(solution)/shard_map/all_gather | solution.py:116
  289.6 57.7 %reduce-scatter.9.cloned.1.call-start = ((), (), s32[]{:S(2)}) async-start(), calls=%async_computation.18 | async-start | bytes 2359296 | tf_op jit(solution)/shard_map/reduce_scatter | solution.py:189
  321.1 55.1 %reduce-scatter.13.cloned.1.call-start = ((), (), s32[]{:S(2)}) async-start(), calls=%async_computation.20 | async-start | bytes 2359296 | tf_op jit(solution)/shard_map/reduce_scatter | solution.py:192
  323.0 82.1 %reduce-scatter.17.cloned.1.call-start = ((), (), s32[]{:S(2)}) async-start(), calls=%async_computation.22 | async-start | bytes 2359296 | tf_op jit(solution)/shard_map/reduce_scatter | solution.py:195
  326.8 249.7 %reduce-scatter.7.cloned.1.call-start = ((), (), s32[]{:S(2)}) async-start(), calls=%async_computation.17 | async-start | bytes 2359296 | tf_op jit(solution)/shard_map/reduce_scatter | solution.py:180
  334.2 323.6 %all-reduce.5.cloned.1.call-start = ((), (), s32[]{:S(2)}) async-start(), calls=%async_computation.23 | async-start | bytes 9437184 | tf_op jit(solution)/shard_map/psum | solution.py:205
  407.8 277.0 %reduce-scatter.11.cloned.1.call-start = ((), (), s32[]{:S(2)}) async-start(), calls=%async_computation.19 | async-start | bytes 2359296 | tf_op jit(solution)/shard_map/reduce_scatter | solution.py:183
  418.0 66.5 %all-to-all-start.2 = ((bf16[4,2,48,2048]{3,2,1,0:T(8,128)(2,1)}), bf16[4,2,48,2048]{3,2,1,0:T(8,128)(2,1)S(1)}, u32[]{:S(2)}, u32[]{:S(2)}) async-start(bf16[4,2,48,2048]{3,2,1,0:T(8,128)(2,1)} %bitcast.113), calls=%async_computation.2 | async-start | bytes 3145728 | tf_op jit(solution)/shard_map/all_to_all | solution.py:143
  484.5 7.6 %copy-start.26 = (bf16[192,384]{1,0:T(8,128)(2,1)S(1)}, bf16[192,384]{1,0:T(8,128)(2,1)}, u32[]{:S(2)}) copy-start(bf16[192,384]{1,0:T(8,128)(2,1)} %get-tuple-element.38) | copy-start | bytes 442372
  484.5 75.3 %all-to-all-start.6 = ((bf16[4,2,48,2048]{3,2,1,0:T(8,128)(2,1)}), bf16[4,2,48,2048]{3,2,1,0:T(8,128)(2,1)S(1)}, u32[]{:S(2)}, u32[]{:S(2)}) async-start(bf16[4,2,48,2048]{3,2,1,0:T(8,128)(2,1)} %bitcast.110), calls=%async_computation.6 | async-start | bytes 3145728 | tf_op jit(solution)/shard_map/all_to_all | solution.py:152
  492.0 221.2 %reduce-scatter.15.cloned.1.call-start = ((), (), s32[]{:S(2)}) async-start(), calls=%async_computation.21 | async-start | bytes 2359296 | tf_op jit(solution)/shard_map/reduce_scatter | solution.py:186
  559.7 6.2 all-to-all-start.3
  565.9 6.2 all-to-all-start.7
  657.8 27.1 %copy-start.18 = (bf16[1024,384]{1,0:T(8,128)(2,1)S(1)}, bf16[1024,384]{1,0:T(8,128)(2,1)}, u32[]{:S(2)}) copy-start(bf16[1024,384]{1,0:T(8,128)(2,1)} %get-tuple-element.8) | copy-start | bytes 2359300
  684.8 28.5 %copy-start.16 = (bf16[384,1024]{1,0:T(8,128)(2,1)S(1)}, bf16[384,1024]{1,0:T(8,128)(2,1)}, u32[]{:S(2)}) copy-start(bf16[384,1024]{1,0:T(8,128)(2,1)} %get-tuple-element.10) | copy-start | bytes 2359300
  684.8 28.5 %copy-start.17 = (bf16[384,1024]{1,0:T(8,128)(2,1)S(1)}, bf16[384,1024]{1,0:T(8,128)(2,1)}, u32[]{:S(2)}) copy-start(bf16[384,1024]{1,0:T(8,128)(2,1)} %get-tuple-element.11) | copy-start | bytes 2359300
  (26 other events, 60.1 us)
Sparse Core Ops, SparseCore 0:
  15.9 209.7 all-reduce.6
  228.2 26.0 all-gather.3
  255.9 27.2 all-gather.5
  289.7 26.2 all-gather.7
  321.2 26.0 reduce-scatter.8
  350.1 26.0 reduce-scatter.12
  379.0 26.0 reduce-scatter.16
  407.5 26.0 reduce-scatter.6
  437.0 220.7 all-reduce.4
  659.8 24.9 reduce-scatter.10
  687.1 26.0 reduce-scatter.14
where the time goes:
time: 724 us; the launch traced here: 723 us
  waiting for transfers between devices  566 us (78%)
  starting transfers between devices  39.5 us (5%)
  matrix products  37.5 us (5%)
  other arithmetic  32.9 us (5%)
  local copies, waits for them, and re-layouts  28.9 us (4%)
  between operations  18 us (2%)
    psum x1, waiting for transfers between devices, broadcast(): return lax.psum(kept, axis)  199 us
    psum x1, waiting for transfers between devices, on_device(): lax.psum(second_slots[0].astype(jnp.bfloat16), 'expert').astype(jnp.float32)  81.3 us
    all_to_all x1, waiting for transfers between devices, on_device(): lax.all_to_all(grad_all.astype(jnp.bfloat16), 'expert', split_axis=0, con...  62.2 us
    all_to_all x1, waiting for transfers between devices, on_device(): lax.all_to_all(out_all.astype(jnp.bfloat16), 'expert', split_axis=0, conc...  55.1 us
    all_to_all x1, waiting for transfers between devices, on_device(): lax.all_to_all(both_scaled, 'expert', split_axis=0, concat_axis=0, tiled=...  32.1 us
    reduce_scatter x1, waiting for transfers between devices, on_device(): lax.psum_scatter(copy_parts[2].astype(jnp.bfloat16), 'dp', scatter_dimens...  26.4 us
    reduce_scatter x1, waiting for transfers between devices, on_device(): lax.psum_scatter(copy_parts[1].astype(jnp.bfloat16), 'dp', scatter_dimens...  26.2 us
    reduce_scatter x1, waiting for transfers between devices, on_device(): lax.psum_scatter(own_parts[2].astype(jnp.bfloat16), 'dp', scatter_dimensi...  25.5 us
  transfers between devices with their start and end apart: 19, of which 14 were waited for; matrix products, arithmetic and copies ran while one was open for 10% of the time, Pallas kernels for 0%

commit v1 on v0

v1 whole, which is shorter than its diff:
```python
import jax
import jax.numpy as jnp
from jax import lax
from jax.sharding import PartitionSpec as P

ACROSS = (((1,), (1,)), ((), ()))
CONTRACT = (((0,), (0,)), ((), ()))
SPLIT_RETURN = False


def dot_f32(left, right, dims=(((1,), (0,)), ((), ()))):
    return lax.dot_general(left, right, dims, preferred_element_type=jnp.float32)


def gather_rows(block):
    return lax.all_gather(block, ("expert", "sub"), axis=0, tiled=True)


def return_rows(part):
    if not SPLIT_RETURN:
        return lax.psum_scatter(part, ("expert", "sub"), scatter_dimension=0, tiled=True)
    experts = lax.axis_size("expert")
    halves = lax.axis_size("sub")
    part = part.reshape(experts, halves, -1, part.shape[-1])
    part = lax.psum_scatter(part, "sub", scatter_dimension=1, tiled=True)
    part = lax.psum_scatter(part, "expert", scatter_dimension=0, tiled=True)
    return part.reshape(-1, part.shape[-1])


def sum_over_dp(part, axis):
    count = lax.axis_size("dp")
    if count != 2:
        return lax.psum_scatter(
            part.astype(jnp.bfloat16), "dp", scatter_dimension=axis, tiled=True
        ).astype(jnp.float32)
    mine = lax.axis_index("dp")
    width = part.shape[axis] // 2
    kept = lax.dynamic_slice_in_dim(part, mine * width, width, axis)
    given = lax.dynamic_slice_in_dim(part, (1 - mine) * width, width, axis)
    came = lax.ppermute(given.astype(jnp.bfloat16), "dp", [(0, 1), (1, 0)])
    return kept.astype(jnp.bfloat16).astype(jnp.float32) + came.astype(jnp.float32)


def on_device(
    tokens,
    cotangent,
    gate_prob,
    target_device,
    use_copy,
    hot_experts,
    copy_slot,
    gate_weight,
    up_weight,
    down_weight,
):
    gate_weight, up_weight, down_weight = gate_weight[0], up_weight[0], down_weight[0]
    copied_expert = hot_experts[copy_slot]
    expert_id = jnp.where(use_copy == 1, copied_expert[target_device], target_device)
    all_ids = gather_rows(expert_id)
    rows = gather_rows(tokens)
    scaled = (gate_prob[:, None] * cotangent.astype(jnp.float32)).astype(jnp.bfloat16)
    scaled_rows = gather_rows(scaled)
    here = (all_ids == lax.axis_index("expert"))[:, None]
    gate_in = dot_f32(rows, gate_weight)
    up_in = dot_f32(rows, up_weight)
    sigmoid_gate = jax.nn.sigmoid(gate_in)
    active = gate_in * sigmoid_gate
    hidden = jnp.where(here, active * up_in, 0.0).astype(jnp.bfloat16)
    expert_out = return_rows(dot_f32(hidden, down_weight).astype(jnp.bfloat16))
    hidden_grad = jnp.where(here, dot_f32(scaled_rows, down_weight, ACROSS), 0.0)
    gate_grad = (
        hidden_grad * up_in * sigmoid_gate * (1.0 + gate_in * (1.0 - sigmoid_gate))
    ).astype(jnp.bfloat16)
    up_grad = (hidden_grad * active).astype(jnp.bfloat16)
    row_grad = dot_f32(gate_grad, gate_weight, ACROSS) + dot_f32(up_grad, up_weight, ACROSS)
    token_grad = return_rows(row_grad.astype(jnp.bfloat16))
    down_sum = sum_over_dp(dot_f32(hidden, scaled_rows, CONTRACT), 1)
    gate_sum = sum_over_dp(dot_f32(rows, gate_grad, CONTRACT), 0)
    up_sum = sum_over_dp(dot_f32(rows, up_grad, CONTRACT), 0)
    out_wide = expert_out.astype(jnp.float32)
    layer_out = (gate_prob[:, None] * out_wide).astype(jnp.bfloat16)
    prob_grad = jnp.sum(cotangent.astype(jnp.float32) * out_wide, axis=1)
    return (layer_out, token_grad, prob_grad, gate_sum[None], up_sum[None], down_sum[None])


def solution(mesh):
    rows = ("groups", "expert", "dp", "sub")
    return jax.shard_map(
        on_device,
        mesh=mesh,
        in_specs=(
            P(rows, None),
            P(rows, None),
            P(rows),
            P(rows),
            P(rows),
            P("groups"),
            P("groups"),
            P("expert", None, "sub"),
            P("expert", None, "sub"),
            P("expert", "sub", None),
        ),
        out_specs=(
            P(rows, None),
            P(rows, None),
            P(rows),
            P(("groups", "expert"), "dp", "sub"),
            P(("groups", "expert"), "dp", "sub"),
            P(("groups", "expert"), "sub", "dp"),
        ),
        check_vma=False,
    )
```

time: 724 us -> 227 us (0.31)
  waiting for transfers between devices: 566 us -> 133 us
  starting transfers between devices: 39.5 us -> 3.83 us
  other arithmetic: 32.9 us -> 13.3 us
  local copies, waits for them, and re-layouts: 28.9 us -> 11.2 us
  blocking collectives: 0 us -> 13.5 us
    psum x2 -> x0, waiting for transfers between devices: 280 us -> none  [the longest x1 199 us: broadcast(): return lax.psum(kept, axis)]
    all_to_all x8 -> x0, waiting for transfers between devices: 153 us -> none  [the longest x1 62.2 us: on_device(): lax.all_to_all(grad_all.astype(jnp.bfloat16), 'expert', split_axis=0, con...]
    reduce_scatter x6 -> x2, waiting for transfers between devices: 115 us -> 26 us  [return_rows(): lax.psum_scatter(part, ('expert', 'sub'), scatter_dimension=0, tiled=True)]
    all_gather x3 -> x2, waiting for transfers between devices: 17.6 us -> 70.4 us  [gather_rows(): return lax.all_gather(block, ('expert', 'sub'), axis=0, tiled=True)]
    all_to_all x8 -> x0, starting transfers between devices: 39 us -> none  [the longest x1 7.56 us: on_device(): lax.all_to_all(grad_all.astype(jnp.bfloat16), 'expert', split_axis=0, con...]
    ppermute x0 -> x3, waiting for transfers between devices: none -> 36.2 us  [sum_over_dp(): came = lax.ppermute(given.astype(jnp.bfloat16), 'dp', [(0, 1), (1, 0)])]
    all_gather x0 -> x1, blocking collectives: none -> 13.5 us  [gather_rows(): return lax.all_gather(block, ('expert', 'sub'), axis=0, tiled=True)]
    all_to_all x6 -> x0, local copies, waits for them, and re-layouts: 12 us -> none  [the longest x1 2.85 us: on_device(): lax.all_to_all(lax.all_to_all(both_scaled, 'expert', split_axis=0, concat...]
  transfers between devices with their start and end apart: 19 -> 7, of which waited for: 14 -> 6; matrix products, arithmetic and copies ran while one was open for 10% -> 20% of each run, Pallas kernels for 0% -> 0%
where the time goes in v1:
time: 227 us; the launch traced here: 226 us
  waiting for transfers between devices  133 us (59%)
  matrix products  37.2 us (16%)
  between operations  14 us (6%)
  blocking collectives  13.5 us (6%)
  other arithmetic  13.3 us (6%)
  local copies, waits for them, and re-layouts  11.2 us (5%)
  starting transfers between devices  3.83 us (2%)
    all_gather x2, waiting for transfers between devices, gather_rows(): return lax.all_gather(block, ('expert', 'sub'), axis=0, tiled=True)  70.4 us
    dot_general x9, matrix products, dot_f32(): lax.dot_general(left, right, dims, preferred_element_type=jnp.float32)  37.2 us
    ppermute x3, waiting for transfers between devices, sum_over_dp(): came = lax.ppermute(given.astype(jnp.bfloat16), 'dp', [(0, 1), (1, 0)])  36.2 us
    reduce_scatter x2, waiting for transfers between devices, return_rows(): lax.psum_scatter(part, ('expert', 'sub'), scatter_dimension=0, tiled=True)  26 us
    all_gather x1, blocking collectives, gather_rows(): return lax.all_gather(block, ('expert', 'sub'), axis=0, tiled=True)  13.5 us
    unnamed x42, local copies, waits for them, and re-layouts  8.03 us
  transfers between devices with their start and end apart: 7, of which 6 were waited for; matrix products, arithmetic and copies ran while one was open for 20% of the time, Pallas kernels for 0%

profile of v1, /device:TPU:0, one launch (start us, length us, event | category | flops | bytes accessed | tf_op | source)
XLA Modules:
  0.0 226.4 jit_solution(18248263074831320622)
XLA Ops:
  8.0 2.0 fusion.14
  11.4 2.6 %fusion.18 = s32[1,1,128]{2,1,0:T(1,128)S(1)} fusion(s32[128]{0:T(128)S(1)} %copy-done.12, s32[128]{0:T(128)S(1)} %copy-done.13, s32[]{:T(128)} %bitcast, s32[]{:T(128)} %bitcast.1, s32[]{:T(128)} %bitcast.2, s32[]{:T(128)} %bitcast.3), kind=kLoop, calls=%fused_computation.45 | loop fusion | flops 1408 | bytes 1552
  14.0 13.5 %all-gather = s32[8,1,128]{2,1,0:T(1,128)S(1)} all-gather(s32[1,1,128]{2,1,0:T(1,128)S(1)} %fusion.18), channel_id=1, replica_groups=mesh['groups'=2,'expert'=4,'dp'=2,'sub'=2] {'expert','sub'}, dimensions={0}, use_global_device_ids=true | all-gather | bytes 4608 | tf_op jit(solution)/shard_map/all_gather | solution.py:16
  27.5 32.1 %all-gather.4.cloned.1.call-done = bf16[1024,2048]{1,0:T(8,128)(2,1)} async-done(((bf16[128,2048]{1,0:T(8,128)(2,1)}), bf16[1024,2048]{1,0:T(8,128)(2,1)}) %all-gather.4.cloned.1.call-update) | async-done | bytes 4194320 | tf_op jit(solution)/shard_map/all_gather | solution.py:16
  59.6 6.3 %fusion.6 = f32[1024,384]{1,0:T(8,128)} fusion(bf16[1024,2048]{1,0:T(8,128)(2,1)} %all-gather.4.cloned.1.call-done, bf16[1,2048,384]{2,1,0:T(8,128)(2,1)} %param.18), kind=kOutput, calls=%fused_computation.11 | convolution fusion | flops 1610612736 | bytes 7340032 | tf_op jit(solution)/shard_map/dot_general | solution.py:12
  65.8 3.5 %fusion.10 = f32[1024,384]{1,0:T(8,128)} fusion(bf16[1024,2048]{1,0:T(8,128)(2,1)S(1)} %copy-done.14, bf16[1,2048,384]{2,1,0:T(8,128)(2,1)S(1)} %copy-done.3), kind=kOutput, calls=%fused_computation.15 | convolution fusion | flops 1610612736 | bytes 7340032 | tf_op jit(solution)/shard_map/dot_general | solution.py:12
  69.3 38.3 %all-gather.6.cloned.1.call-done = bf16[1024,2048]{1,0:T(8,128)(2,1)} async-done(((bf16[128,2048]{1,0:T(8,128)(2,1)}), bf16[1024,2048]{1,0:T(8,128)(2,1)}) %all-gather.6.cloned.1.call-update) | async-done | bytes 4194320 | tf_op jit(solution)/shard_map/all_gather | solution.py:16
  107.6 7.2 %multiply_convert_fusion = (bf16[1024,384]{1,0:T(8,128)(2,1)}, bf16[1024,384]{1,0:T(8,128)(2,1)}, bf16[1024,384]{1,0:T(8,128)(2,1)S(1)}) fusion(pred[1024]{0:T(1024)(128)(4,1)S(1)} %compare_bitcast_fusion, f32[1024,384]{1,0:T(8,128)} %fusion.10, f32[1024,384]{1,0:T(8,128)} %fusion.6, bf16[1024,2048]{1,0:T(8,128)(2,1)} %all-gather.6.cloned.1.call-done, ...), kind=kOutput, calls=%fused_computation.24 | convolution fusion | flops 1617297408 | bytes 11273216 | tf_op jit(solution)/shard_map/dot_general | solution.py:12
  115.8 4.3 %convolution_convert_fusion = bf16[1024,2048]{1,0:T(8,128)(2,1)} fusion(bf16[1024,384]{1,0:T(8,128)(2,1)S(1)} %get-tuple-element.26, bf16[1,384,2048]{2,1,0:T(8,128)(2,1)S(1)} %copy-done), kind=kOutput, calls=%fused_computation.2 | convolution fusion | flops 1612709888 | bytes 6553600 | tf_op jit(solution)/shard_map/dot_general | solution.py:12
  120.3 3.6 %fusion.8 = f32[1024,2048]{1,0:T(8,128)S(1)} fusion(bf16[1024,384]{1,0:T(8,128)(2,1)} %get-tuple-element.25, bf16[1,2048,384]{2,1,0:T(8,128)(2,1)S(1)} %copy-done.3), kind=kOutput, calls=%fused_computation.13 | convolution fusion | flops 1610612736 | bytes 10747904 | tf_op jit(solution)/shard_map/dot_general | solution.py:12
  124.0 4.4 %add_convert_fusion = bf16[1024,2048]{1,0:T(8,128)(2,1)} fusion(f32[1024,2048]{1,0:T(8,128)S(1)} %fusion.8, bf16[1024,384]{1,0:T(8,128)(2,1)S(1)} %copy-done.9, bf16[1,2048,384]{2,1,0:T(8,128)(2,1)S(1)} %copy-done.4), kind=kOutput, calls=%fused_computation.1 | convolution fusion | flops 1614807040 | bytes 14942208 | tf_op jit(solution)/shard_map/dot_general | solution.py:12
  129.5 4.2 %fusion.21 = bf16[384,2048]{1,0:T(8,128)(2,1)S(1)} fusion(bf16[1024,384]{1,0:T(8,128)(2,1)S(1)} %copy-done.10, bf16[1024,2048]{1,0:T(8,128)(2,1)} %all-gather.4.cloned.1.call-done), kind=kOutput, calls=%fused_computation.48 | convolution fusion | flops 1610612736 | bytes 6553600 | tf_op jit(solution)/shard_map/dot_general | solution.py:12
  136.4 1.9 fusion.20
  140.2 1.9 fusion.22
  145.6 9.7 %collective-permute-done.1 = bf16[1024,384]{0,1:T(8,128)(2,1)} collective-permute-done((bf16[1024,384]{0,1:T(8,128)(2,1)S(1)}, bf16[1024,384]{0,1:T(8,128)(2,1)}, u32[]{:S(2)}, u32[]{:S(2)}) %collective-permute-start.1) | collective-permute-done | bytes 786464 | tf_op jit(solution)/shard_map/ppermute | solution.py:40
  155.4 1.7 fusion
  157.0 1.6 copy.22
  158.7 13.6 %collective-permute-done = bf16[1024,384]{0,1:T(8,128)(2,1)} collective-permute-done((bf16[1024,384]{0,1:T(8,128)(2,1)}, bf16[1024,384]{0,1:T(8,128)(2,1)}, u32[]{:S(2)}, u32[]{:S(2)}) %collective-permute-start) | collective-permute-done | bytes 786464 | tf_op jit(solution)/shard_map/ppermute | solution.py:40
  172.2 1.6 fusion.1
  173.9 1.6 copy.21
  175.5 12.9 %collective-permute-done.2 = bf16[384,1024]{1,0:T(8,128)(2,1)} collective-permute-done((bf16[384,1024]{1,0:T(8,128)(2,1)}, bf16[384,1024]{1,0:T(8,128)(2,1)}, u32[]{:S(2)}, u32[]{:S(2)}) %collective-permute-start.2) | collective-permute-done | bytes 786464 | tf_op jit(solution)/shard_map/ppermute | solution.py:40
  188.4 2.8 %add_bitcast_fusion = f32[1,384,1024]{2,1,0:T(8,128)} fusion(bf16[384,1024]{1,0:T(8,128)(2,1)} %collective-permute-done.2, bf16[384,2048]{1,0:T(8,128)(2,1)} %copy-done.5, s32[]{:T(128)S(6)} %select_n.32), kind=kLoop, calls=%fused_computation.17 | loop fusion | flops 1179648 | bytes 3145732 | tf_op jit(solution)/shard_map/broadcast_in_dim | solution.py:83
  191.2 2.6 %fusion.15 = (f32[128]{0:T(128)}, bf16[128,2048]{1,0:T(8,128)(2,1)}) fusion(bf16[128,2048]{1,0:T(8,128)(2,1)} %reduce-scatter.3.cloned.1.call-done, bf16[128,2048]{1,0:T(8,128)(2,1)S(1)} %copy-done.2, f32[128]{0:T(128)S(1)} %copy-done.11), kind=kLoop, calls=%fused_computation.34 | loop fusion | flops 1572736 | bytes 1573888 | tf_op jit(solution)/shard_map/reduce_sum | solution.py:82
  193.8 26.0 %reduce-scatter.5.cloned.1.call-done = bf16[128,2048]{1,0:T(8,128)(2,1)} async-done(((bf16[1024,2048]{1,0:T(8,128)(2,1)}), bf16[128,2048]{1,0:T(8,128)(2,1)}) %reduce-scatter.5.cloned.1.call-update) | async-done | bytes 524304 | tf_op jit(solution)/shard_map/reduce_scatter | solution.py:21
  (60 shorter events, 12.5 us)
Async XLA Ops:
  7.2 100.5 %copy-start = (bf16[1,384,2048]{2,1,0:T(8,128)(2,1)S(1)}, bf16[1,384,2048]{2,1,0:T(8,128)(2,1)}, u32[]{:S(2)}) copy-start(bf16[1,384,2048]{2,1,0:T(8,128)(2,1)} %param.19) | copy-start | bytes 4718596
  7.2 2.9 %copy-start.17 = (s32[4]{0:T(128)S(1)}, s32[4]{0:T(128)}, u32[]{:S(2)}) copy-start(s32[4]{0:T(128)} %param.16) | copy-start | bytes 52
  7.2 2.9 %copy-start.1 = (s32[2]{0:T(128)S(1)}, s32[2]{0:T(128)}, u32[]{:S(2)}) copy-start(s32[2]{0:T(128)} %param.15) | copy-start | bytes 28
  7.2 4.2 %copy-start.13 = (s32[128]{0:T(128)S(1)}, s32[128]{0:T(128)}, u32[]{:S(2)}) copy-start(s32[128]{0:T(128)} %param.14) | copy-start | bytes 1540
  7.2 4.1 %copy-start.12 = (s32[128]{0:T(128)S(1)}, s32[128]{0:T(128)}, u32[]{:S(2)}) copy-start(s32[128]{0:T(128)} %param.13) | copy-start | bytes 1540
  7.2 52.3 %all-gather.4.cloned.1.call-start = ((), (), s32[]{:S(2)}) async-start(), calls=%async_computation.2 | async-start | bytes 4718592 | tf_op jit(solution)/shard_map/all_gather | solution.py:16
  8.0 99.7 %all-gather.6.cloned.1.call-start = ((), (), s32[]{:S(2)}) async-start(), calls=%async_computation.4 | async-start | bytes 4718592 | tf_op jit(solution)/shard_map/all_gather | solution.py:16
  10.0 181.2 %reduce-scatter.3.cloned.1.call-start = ((), (), s32[]{:S(2)}) async-start(), calls=%async_computation.3 | async-start | bytes 4718592 | tf_op jit(solution)/shard_map/reduce_scatter | solution.py:21
  27.5 38.4 %copy-start.3 = (bf16[1,2048,384]{2,1,0:T(8,128)(2,1)S(1)}, bf16[1,2048,384]{2,1,0:T(8,128)(2,1)}, u32[]{:S(2)}) copy-start(bf16[1,2048,384]{2,1,0:T(8,128)(2,1)} %param.17) | copy-start | bytes 4718596
  59.5 6.3 %copy-start.14 = (bf16[1024,2048]{1,0:T(8,128)(2,1)S(1)}, bf16[1024,2048]{1,0:T(8,128)(2,1)}, u32[]{:S(2)}) copy-start(bf16[1024,2048]{1,0:T(8,128)(2,1)} %all-gather.4.cloned.1.call-done) | copy-start | bytes 12582916
  120.1 99.8 %reduce-scatter.5.cloned.1.call-start = ((), (), s32[]{:S(2)}) async-start(), calls=%async_computation.5 | async-start | bytes 4718592 | tf_op jit(solution)/shard_map/reduce_scatter | solution.py:21
  120.3 3.7 %copy-start.4 = (bf16[1,2048,384]{2,1,0:T(8,128)(2,1)S(1)}, bf16[1,2048,384]{2,1,0:T(8,128)(2,1)}, u32[]{:S(2)}) copy-start(bf16[1,2048,384]{2,1,0:T(8,128)(2,1)} %param.18) | copy-start | bytes 4718596
  120.3 3.7 %copy-start.9 = (bf16[1024,384]{1,0:T(8,128)(2,1)S(1)}, bf16[1024,384]{1,0:T(8,128)(2,1)}, u32[]{:S(2)}) copy-start(bf16[1024,384]{1,0:T(8,128)(2,1)} %get-tuple-element.24) | copy-start | bytes 2359300
  129.5 6.8 %copy-start.15 = (bf16[1024,2048]{1,0:T(8,128)(2,1)S(1)}, bf16[1024,2048]{1,0:T(8,128)(2,1)}, u32[]{:S(2)}) copy-start(bf16[1024,2048]{1,0:T(8,128)(2,1)} %all-gather.4.cloned.1.call-done) | copy-start | bytes 12582916
  133.8 2.6 %copy-start.8 = (bf16[1024,384]{1,0:T(8,128)(2,1)S(1)}, bf16[1024,384]{1,0:T(8,128)(2,1)}, u32[]{:S(2)}) copy-start(bf16[1024,384]{1,0:T(8,128)(2,1)} %get-tuple-element.25) | copy-start | bytes 2359300
  134.9 20.5 %collective-permute-start.1 = (bf16[1024,384]{0,1:T(8,128)(2,1)S(1)}, bf16[1024,384]{0,1:T(8,128)(2,1)}, u32[]{:S(2)}, u32[]{:S(2)}) collective-permute-start(bf16[1024,384]{0,1:T(8,128)(2,1)S(1)} %fusion.17), channel_id=1, source_target_pairs={{0,2},{2,0},{1,3},{3,1},{4,6},{6,4},{5,7},{7,5},{8,10},{10,8},{9,1... | collective-permute-start | bytes 2359304 | tf_op jit(solution)/shard_map/ppermute | solution.py:40
  136.4 3.8 %copy-start.16 = (bf16[1024,2048]{1,0:T(8,128)(2,1)S(1)}, bf16[1024,2048]{1,0:T(8,128)(2,1)}, u32[]{:S(2)}) copy-start(bf16[1024,2048]{1,0:T(8,128)(2,1)} %all-gather.6.cloned.1.call-done) | copy-start | bytes 12582916
  138.2 1.4 copy-start.6
  138.2 2.0 copy-start.19
  139.6 32.6 %collective-permute-start = (bf16[1024,384]{0,1:T(8,128)(2,1)}, bf16[1024,384]{0,1:T(8,128)(2,1)}, u32[]{:S(2)}, u32[]{:S(2)}) collective-permute-start(bf16[1024,384]{0,1:T(8,128)(2,1)} %fusion.16), channel_id=1, source_target_pairs={{0,2},{2,0},{1,3},{3,1},{4,6},{6,4},{5,7},{7,5},{8,10},{10,8},{9,1... | collective-permute-start | bytes 2359304 | tf_op jit(solution)/shard_map/ppermute | solution.py:40
  142.1 1.2 copy-start.5
  144.2 44.2 %collective-permute-start.2 = (bf16[384,1024]{1,0:T(8,128)(2,1)}, bf16[384,1024]{1,0:T(8,128)(2,1)}, u32[]{:S(2)}, u32[]{:S(2)}) collective-permute-start(bf16[384,1024]{1,0:T(8,128)(2,1)} %dynamic-slice_convert_fusion), channel_id=1, source_target_pairs={{0,2},{2,0},{1,3},{3,1},{4,6},{6,4},{5,7},{7,5},{8,10},{10,8},{9,1... | collective-permute-start | bytes 2359304 | tf_op jit(solution)/shard_map/ppermute | solution.py:40
  175.5 15.7 %copy-start.2 = (bf16[128,2048]{1,0:T(8,128)(2,1)S(1)}, bf16[128,2048]{1,0:T(8,128)(2,1)}, u32[]{:S(2)}) copy-start(bf16[128,2048]{1,0:T(8,128)(2,1)} %param.11) | copy-start | bytes 1572868
  175.5 15.7 %copy-start.11 = (f32[128]{0:T(128)S(1)}, f32[128]{0:T(128)}, u32[]{:S(2)}) copy-start(f32[128]{0:T(128)} %param.12) | copy-start | bytes 1540
  (3 other events, 3.2 us)
Sparse Core Ops, SparseCore 0:
  9.7 49.8 all-gather.3
  61.7 45.8 all-gather.5
  120.2 48.7 reduce-scatter.2
  171.7 48.1 reduce-scatter.4

commit v2 on v1

--- a/solution.py
+++ b/solution.py
@@ -1,6 +1,10 @@
+import functools
+
 import jax
 import jax.numpy as jnp
 from jax import lax
+from jax.experimental import pallas as pl
+from jax.experimental.pallas import tpu as pltpu
 from jax.sharding import PartitionSpec as P
 
 ACROSS = (((1,), (1,)), ((), ()))
@@ -10,6 +14,364 @@
 
 def dot_f32(left, right, dims=(((1,), (0,)), ((), ()))):
     return lax.dot_general(left, right, dims, preferred_element_type=jnp.float32)
+
+
+MESH = pl.DeviceIdType.MESH
+LANES = 128
+TILE = 512
+
+
+def fused_kernel(
+    n,
+    tok_own,
+    sca_own,
+    gate_w,
+    up_w,
+    down_w,
+    rows_out,
+    kept_gate,
+    kept_up,
+    kept_down,
+    came_gate,
+    came_up,
+    came_down,
+    tok,
+    sca,
+    part,
+    sib_in,
+    z_in,
+    hidden_s,
+    gate_s,
+    up_s,
+    given_gate,
+    given_up,
+    given_down,
+    z_send,
+    z_recv,
+    sib_send,
+    sib_recv,
+    part_send,
+    part_recv,
+    ret_send,
+    ret_recv,
+    dp_send,
+    dp_recv,
+):
+    me = lax.axis_index("expert")
+    sub = lax.axis_index("sub")
+    dp = lax.axis_index("dp")
+    other = 1 - sub
+    last = n - 1
+    count = tok_own.shape[0]
+    width = sca_own.shape[1]
+    half = width // 2
+    both = 2 * count
+    has_left = me > 0
+    has_right = me < last
+
+    def remote(src, dst, send, recv, where):
+        return pltpu.make_async_remote_copy(
+            src_ref=src,
+            dst_ref=dst,
+            send_sem=send,
+            recv_sem=recv,
+            device_id=where,
+            device_id_type=MESH,
+        )
+
+    held = (tok, sca)
+
+    def toward(side):
+        return {"expert": me + 1 - 2 * side}
+
+    def z_copy(kind, side, step, block):
+        ref = held[kind].at[block, sub]
+        return remote(
+            ref, ref, z_send.at[kind, side, step], z_recv.at[kind, side, step], toward(side)
+        )
+
+    def sib_copy(kind, block, row):
+        ref = held[kind].at[block, row]
+        return remote(
+            ref, ref, sib_send.at[kind, block], sib_recv.at[kind, block], {"sub": other}
+        )
+
+    def part_copy(block, kind):
+        return remote(
+            part.at[block, kind, other],
+            sib_in.at[block, kind],
+            part_send.at[block, kind],
+            part_recv.at[block, kind],
+            {"sub": other},
+        )
+
+    def ret_copy(side, dest, slot, kind):
+        return remote(
+            part.at[dest, kind, sub],
+            z_in.at[slot, kind],
+            ret_send.at[dest, kind],
+            ret_recv.at[slot, kind],
+            toward(side),
+        )
+
+    barrier = pltpu.get_barrier_semaphore()
+
+    @pl.when(has_left)
+    def _():
+        pl.semaphore_signal(barrier, inc=1, device_id={"expert": me - 1}, device_id_type=MESH)
+
+    @pl.when(has_right)
+    def _():
+        pl.semaphore_signal(barrier, inc=1, device_id={"expert": me + 1}, device_id_type=MESH)
+
+    pl.semaphore_signal(barrier, inc=1, device_id={"sub": other}, device_id_type=MESH)
+    pl.semaphore_signal(barrier, inc=1, device_id={"dp": 1 - dp}, device_id_type=MESH)
+    tok[me, sub] = tok_own[...]
+    sca[me, sub] = sca_own[...]
+    pl.semaphore_wait(barrier, 2 + has_left.astype(jnp.int32) + has_right.astype(jnp.int32))
+
+    for kind in range(2):
+
+        @pl.when(has_right)
+        def _():
+            z_copy(kind, 0, 0, me).start()
+
+        @pl.when(has_left)
+        def _():
+            z_copy(kind, 1, 0, me).start()
+
+        sib_copy(kind, me, sub).start()
+
+    def arrivals(step):
+        for kind in range(2):
+            for side in range(2):
+                block = me - 1 - step if side == 0 else me + 1 + step
+                valid = block >= 0 if side == 0 else block <= last
+                onward = has_right if side == 0 else has_left
+
+                @pl.when(valid)
+                def _():
+                    z_copy(kind, side, step, block).wait_recv()
+                    sib_copy(kind, block, sub).start()
+
+                    @pl.when(onward)
+                    def _():
+                        z_copy(kind, side, step + 1, block).start()
+
+    def compute(block):
+        sib_copy(0, block, other).wait_recv()
+        x = tok[block, :, :, :width].reshape(both, width)
+        here = tok[block, :, :, width:].reshape(both, LANES).astype(jnp.float32)
+        here = here[:, :1] == me.astype(jnp.float32)
+        gate_in = dot_f32(x, gate_w[...])
+        up_in = dot_f32(x, up_w[...])
+        sigmoid_gate = 1.0 / (1.0 + jnp.exp(-gate_in))
+        active = gate_in * sigmoid_gate
+        hidden = jnp.where(here, active * up_in, 0.0).astype(jnp.bfloat16)
+        slope = up_in * sigmoid_gate * (1.0 + gate_in * (1.0 - sigmoid_gate))
+        place = pl.ds(pl.multiple_of(block * both, both), both)
+        hidden_s[place, :] = hidden
+
+        @pl.loop(0, width // TILE)
+        def _(tile):
+            cols = pl.ds(pl.multiple_of(tile * TILE, TILE), TILE)
+            piece = dot_f32(hidden_s[place, :], down_w[:, cols]).astype(jnp.bfloat16)
+            part[block, 0, :, :, cols] = piece.reshape(2, count, TILE)
+
+        part_copy(block, 0).start()
+        sib_copy(1, block, other).wait_recv()
+        s = sca[block].reshape(both, width)
+        hidden_grad = jnp.where(here, dot_f32(s, down_w[...], ACROSS), 0.0)
+        gate_s[place, :] = (hidden_grad * slope).astype(jnp.bfloat16)
+        up_s[place, :] = (hidden_grad * active).astype(jnp.bfloat16)
+
+        @pl.loop(0, width // TILE)
+        def _(tile):
+            rows = pl.ds(pl.multiple_of(tile * TILE, TILE), TILE)
+            piece = dot_f32(gate_s[place, :], gate_w[rows, :], ACROSS)
+            piece = piece + dot_f32(up_s[place, :], up_w[rows, :], ACROSS)
+            part[block, 1, :, :, rows] = piece.astype(jnp.bfloat16).reshape(2, count, TILE)
+
+        part_copy(block, 1).start()
+
+    def add_sibling(dest, kind):
+        part_copy(dest, kind).wait_recv()
+        mine = part[dest, kind, sub].astype(jnp.float32)
+        return mine + sib_in[dest, kind].astype(jnp.float32)
+
+    def sends(turn):
+        right = turn + 1 - me
+        left = last - (turn + 1 - (last - me))
+        return (
+            (0, right, (right > me) & (right <= last), has_left, right),
+            (1, left, (left < me) & (left >= 0), has_right, jnp.where(left == me - 1, n, left)),
+        )
+
+    def give_back(turn):
+        for kind in range(2):
+            for side, dest, valid, add, slot in sends(turn):
+
+                @pl.when(valid)
+                def _():
+                    part[dest, kind, sub] = add_sibling(dest, kind).astype(jnp.bfloat16)
+
+                    @pl.when(add)
+                    def _():
+                        ret_copy(side, dest, dest, kind).wait_recv()
+                        part[dest, kind, sub] = (
+                            part[dest, kind, sub].astype(jnp.float32)
+                            + z_in[dest, kind].astype(jnp.float32)
+                        ).astype(jnp.bfloat16)
+
+                    ret_copy(side, dest, slot, kind).start()
+
+    @pl.loop(0, n)
+    def _(time):
+        step = time - 1
+
+        @pl.when(time > 0)
+        def _():
+            arrivals(step)
+
+        @pl.loop(0, 2)
+        def _(side):
+            block = jnp.where(side == 0, me - time, me + time)
+            valid = (block >= 0) & (block <= last) & ((time > 0) | (side == 0))
+
+            @pl.when(valid)
+            def _():
+                compute(block)
+
+        @pl.when(time > 0)
+        def _():
+            give_back(step)
+
+    given = (given_gate, given_up, given_down)
+    kept = (kept_gate, kept_up, kept_down)
+    came = (came_gate, came_up, came_down)
+
+    def dp_copy(kind):
+        return remote(
+            given[kind], came[kind], dp_send.at[kind], dp_recv.at[kind], {"dp": 1 - dp}
+        )
+
+    total = n * both
+
+    def weight_grad(kind, first, into):
+        if kind < 2:
+            right_ref = (gate_s, up_s)[kind]
+
+            @pl.loop(0, half // TILE)
+            def _(tile):
+                cols = pl.ds(pl.multiple_of(first + tile * TILE, TILE), TILE)
+                rows = pl.ds(pl.multiple_of(tile * TILE, TILE), TILE)
+                x = tok[:, :, :, cols].reshape(total, TILE)
+                into[rows, :] = dot_f32(x, right_ref[...], CONTRACT).astype(jnp.bfloat16)
+
+        else:
+
+            @pl.loop(0, half // TILE)
+            def _(tile):
+                cols = pl.ds(pl.multiple_of(first + tile * TILE, TILE), TILE)
+                there = pl.ds(pl.multiple_of(tile * TILE, TILE), TILE)
+                s = sca[:, :, :, cols].reshape(total, TILE)
+                into[:, there] = dot_f32(hidden_s[...], s, CONTRACT).astype(jnp.bfloat16)
+
+    for kind in range(3):
+        weight_grad(kind, (1 - dp) * half, given[kind])
+        dp_copy(kind).start()
+
+    @pl.loop(n - 1, 2 * n - 3)
+    def _(turn):
+        give_back(turn)
+
+    for kind in range(3):
+        weight_grad(kind, dp * half, kept[kind])
+
+    for kind in range(2):
+        rows_out[kind] = add_sibling(me, kind).astype(jnp.bfloat16)
+        for slot, valid in ((me, has_left), (n, has_right)):
+
+            @pl.when(valid)
+            def _():
+                ret_copy(0, me, slot, kind).wait_recv()
+                rows_out[kind] = (
+                    rows_out[kind].astype(jnp.float32) + z_in[slot, kind].astype(jnp.float32)
+                ).astype(jnp.bfloat16)
+
+    @pl.loop(0, n)
+    def _(block):
+        for kind in range(2):
+            sib_copy(kind, block, sub).wait_send()
+            part_copy(block, kind).wait_send()
+
+            @pl.when(block != me)
+            def _():
+                ret_copy(0, block, block, kind).wait_send()
+
+    @pl.loop(0, n - 1)
+    def _(step):
+        for kind in range(2):
+
+            @pl.when(has_right & (me - step >= 0))
+            def _():
+                z_copy(kind, 0, step, me).wait_send()
+
+            @pl.when(has_left & (me + step <= last))
+            def _():
+                z_copy(kind, 1, step, me).wait_send()
+
+    for kind in range(3):
+        dp_copy(kind).wait()
+
+
+def fused(tok_own, sca_own, gate_weight, up_weight, down_weight):
+    n = lax.axis_size("expert")
+    count, width = sca_own.shape
+    hidden_width = gate_weight.shape[1]
+    half = width // 2
+    b16 = jnp.bfloat16
+    vmem = pl.BlockSpec(memory_space=pltpu.VMEM)
+    hbm = pl.BlockSpec(memory_space=pl.ANY)
+    tall = jax.ShapeDtypeStruct((half, hidden_width), b16)
+    wide = jax.ShapeDtypeStruct((hidden_width, half), b16)
+    dma = pltpu.SemaphoreType.DMA
+    flops = 2 * 9 * n * 2 * count * width * hidden_width
+    return pl.pallas_call(
+        functools.partial(fused_kernel, n),
+        out_shape=(
+            jax.ShapeDtypeStruct((2, count, width), b16), tall, tall, wide, tall, tall, wide,
+        ),
+        in_specs=[vmem] * 5,
+        out_specs=(vmem, vmem, vmem, vmem, hbm, hbm, hbm),
+        scratch_shapes=[
+            pltpu.VMEM((n, 2, count, width + LANES), b16),
+            pltpu.VMEM((n, 2, count, width), b16),
+            pltpu.VMEM((n, 2, 2, count, width), b16),
+            pltpu.VMEM((n, 2, count, width), b16),
+            pltpu.VMEM((n + 1, 2, count, width), b16),
+            pltpu.VMEM((n * 2 * count, hidden_width), b16),
+            pltpu.VMEM((n * 2 * count, hidden_width), b16),
+            pltpu.VMEM((n * 2 * count, hidden_width), b16),
+            pltpu.VMEM((half, hidden_width), b16),
+            pltpu.VMEM((half, hidden_width), b16),
+            pltpu.VMEM((hidden_width, half), b16),
+            dma((2, 2, n)),
+            dma((2, 2, n)),
+            dma((2, n)),
+            dma((2, n)),
+            dma((n, 2)),
+            dma((n, 2)),
+            dma((n, 2)),
+            dma((n + 1, 2)),
+            dma((3,)),
+            dma((3,)),
+        ],
+        compiler_params=pltpu.CompilerParams(
+            collective_id=0, has_side_effects=True, vmem_limit_bytes=60 * 2**20
+        ),
+        cost_estimate=pl.CostEstimate(flops=flops, bytes_accessed=2**24, transcendentals=0),
+    )(tok_own, sca_own, gate_weight, up_weight, down_weight)
 
 
 def gather_rows(block):
@@ -41,24 +403,9 @@
     return kept.astype(jnp.bfloat16).astype(jnp.float32) + came.astype(jnp.float32)
 
 
-def on_device(
-    tokens,
-    cotangent,
-    gate_prob,
-    target_device,
-    use_copy,
-    hot_experts,
-    copy_slot,
-    gate_weight,
-    up_weight,
-    down_weight,
-):
-    gate_weight, up_weight, down_weight = gate_weight[0], up_weight[0], down_weight[0]
-    copied_expert = hot_experts[copy_slot]
-    expert_id = jnp.where(use_copy == 1, copied_expert[target_device], target_device)
+def gathered(tokens, scaled, expert_id, gate_weight, up_weight, down_weight):
     all_ids = gather_rows(expert_id)
     rows = gather_rows(tokens)
-    scaled = (gate_prob[:, None] * cotangent.astype(jnp.float32)).astype(jnp.bfloat16)
     scaled_rows = gather_rows(scaled)
     here = (all_ids == lax.axis_index("expert"))[:, None]
     gate_in = dot_f32(rows, gate_weight)
@@ -77,6 +424,40 @@
     down_sum = sum_over_dp(dot_f32(hidden, scaled_rows, CONTRACT), 1)
     gate_sum = sum_over_dp(dot_f32(rows, gate_grad, CONTRACT), 0)
     up_sum = sum_over_dp(dot_f32(rows, up_grad, CONTRACT), 0)
+    return expert_out, token_grad, gate_sum, up_sum, down_sum
+
+
+def on_device(
+    tokens,
+    cotangent,
+    gate_prob,
+    target_device,
+    use_copy,
+    hot_experts,
+    copy_slot,
+    gate_weight,
+    up_weight,
+    down_weight,
+):
+    gate_weight, up_weight, down_weight = gate_weight[0], up_weight[0], down_weight[0]
+    copied_expert = hot_experts[copy_slot]
+    expert_id = jnp.where(use_copy == 1, copied_expert[target_device], target_device)
+    scaled = (gate_prob[:, None] * cotangent.astype(jnp.float32)).astype(jnp.bfloat16)
+    if lax.axis_size("expert") <= 4 and lax.axis_size("dp") == 2 and lax.axis_size("sub") == 2:
+        meta = jnp.broadcast_to(
+            expert_id.astype(jnp.bfloat16)[:, None], (tokens.shape[0], LANES)
+        )
+        packed = jnp.concatenate((tokens, meta), axis=1)
+        back, *grads = fused(packed, scaled, gate_weight, up_weight, down_weight)
+        expert_out, token_grad = back[0], back[1]
+        gate_sum, up_sum, down_sum = (
+            kept.astype(jnp.float32) + came.astype(jnp.float32)
+            for kept, came in zip(grads[:3], grads[3:])
+        )
+    else:
+        expert_out, token_grad, gate_sum, up_sum, down_sum = gathered(
+            tokens, scaled, expert_id, gate_weight, up_weight, down_weight
+        )
     out_wide = expert_out.astype(jnp.float32)
     layer_out = (gate_prob[:, None] * out_wide).astype(jnp.bfloat16)
     prob_grad = jnp.sum(cotangent.astype(jnp.float32) * out_wide, axis=1)

time: 227 us -> 157 us (0.69)
  Pallas kernels: 0 us -> 141 us
  waiting for transfers between devices: 133 us -> 0 us
  matrix products: 37.2 us -> 0 us
  blocking collectives: 13.5 us -> 0 us
  between operations: 14 us -> 0.69 us
  local copies, waits for them, and re-layouts: 11.2 us -> 2.17 us
  starting transfers between devices: 3.83 us -> 0 us
    pallas_call x0 -> x1, Pallas kernels: none -> 141 us  [fused(): pl.pallas_call(functools.partial(fused_kernel, n), out_shape=(jax.ShapeDt...]
    all_gather x2 -> x0, waiting for transfers between devices: 70.4 us -> none  [gather_rows(): return lax.all_gather(block, ('expert', 'sub'), axis=0, tiled=True)]
    dot_general x9 -> x0, matrix products: 37.2 us -> none  [dot_f32(): lax.dot_general(left, right, dims, preferred_element_type=jnp.float32)]
    ppermute x3 -> x0, waiting for transfers between devices: 36.2 us -> none  [sum_over_dp(): came = lax.ppermute(given.astype(jnp.bfloat16), 'dp', [(0, 1), (1, 0)])]
    reduce_scatter x2 -> x0, waiting for transfers between devices: 26 us -> none  [return_rows(): lax.psum_scatter(part, ('expert', 'sub'), scatter_dimension=0, tiled=True)]
    all_gather x1 -> x0, blocking collectives: 13.5 us -> none  [gather_rows(): return lax.all_gather(block, ('expert', 'sub'), axis=0, tiled=True)]
    unnamed x42 -> x12, local copies, waits for them, and re-layouts: 8.03 us -> 0.03 us
    ppermute x3 -> x0, starting transfers between devices: 3.49 us -> none  [sum_over_dp(): came = lax.ppermute(given.astype(jnp.bfloat16), 'dp', [(0, 1), (1, 0)])]
  transfers between devices with their start and end apart: 7 -> 0, of which waited for: 6 -> 0; matrix products, arithmetic and copies ran while one was open for 20% -> 0% of each run, Pallas kernels for 0% -> 0%
where the time goes in v2:
time: 157 us
  Pallas kernels  141 us (90%)
  other arithmetic  13.7 us (9%)
  local copies, waits for them, and re-layouts  2.17 us (1%)
    pallas_call x1, Pallas kernels, fused(): pl.pallas_call(functools.partial(fused_kernel, n), out_shape=(jax.ShapeDt...  141 us
    broadcast_in_dim x1, other arithmetic, on_device(): up_sum[None]  3.9 us
    convert_element_type x1, other arithmetic, on_device(): expert_id.astype(jnp.bfloat16)[:, None]  3.27 us

profile of v2, /device:TPU:0, one launch (start us, length us, event | category | flops | bytes accessed | tf_op | source)
XLA Modules:
  0.0 157.2 jit_solution(11083987704649100882)
XLA Ops:
  0.6 0.0 copy-start
  0.6 0.0 copy-start.5
  0.7 0.0 copy-start.1
  0.7 0.7 compare_select_fusion.1
  1.4 0.0 copy-done
  1.4 0.6 gather_fusion
  2.0 0.6 fusion.4
  2.6 3.3 %fusion.3 = bf16[128]{0:T(256)(128)(2,1)S(1)} fusion(s32[128]{0:T(128)} %param.13, s32[128]{0:T(128)} %param.14, s32[]{:T(128)} %bitcast, s32[]{:T(128)} %bitcast.1, s32[]{:T(128)} %bitcast.2, s32[]{:T(128)} %bitcast.3), kind=kLoop, calls=%fused_computation.19 | loop fusion | flops 1536 | bytes 1296 | tf_op jit(solution)/shard_map/convert_element_type | solution.py:448
  5.9 0.1 broadcast_in_dim.25
  6.0 1.9 %pad_maximum_fusion.tok_own = bf16[128,2176]{1,0:T(8,128)(2,1)} fusion(bf16[128,128]{1,0:T(8,128)(2,1)S(1)} %broadcast_in_dim.25, bf16[128,2048]{1,0:T(8,128)(2,1)} %param.10), kind=kLoop, calls=%fused_computation.10 | loop fusion | flops 1114112 | bytes 1114112 | tf_op jit(solution)/shard_map/concatenate | solution.py:450
  7.9 0.0 copy-done.5
  7.9 0.0 copy-done.1
  7.9 0.9 fusion.sca_own
  8.8 140.6 %shard_map.145 = (bf16[2,128,2048]{2,1,0:T(8,128)(2,1)}, bf16[1024,384]{1,0:T(8,128)(2,1)}, bf16[1024,384]{1,0:T(8,128)(2,1)}, bf16[384,1024]{1,0:T(8,128)(2,1)}...) custom-call(bf16[128,2176]{1,0:T(8,128)(2,1)} %pad_maximum_fusion.tok_own, ...), custom_call_target="tpu_custom_call" | custom-call | flops 14495514624 | bytes 16777216 | tf_op jit(solution)/shard_map/pallas_call | solution.py:340
  149.5 0.0 copy-start.2
  149.5 3.9 %add_bitcast_fusion.1 = (f32[1,1024,384]{2,1,0:T(8,128)}, f32[1,1024,384]{2,1,0:T(8,128)}) fusion(bf16[1024,384]{1,0:T(8,128)(2,1)} %get-tuple-element.17, bf16[1024,384]{1,0:T(8,128)(2,1)} %get-tuple-element.16, bf16[1024,384]{1,0:T(8,128)(2,1)} %get-tuple-element.15, bf16[1024,384]{1,0:T(8,128)(2,1)} %get-tuple-element.14), kind=kLoop, calls=%fused_computation.2 | loop fusion | flops 2359296 | bytes 6291456 | tf_op jit(solution)/shard_map/broadcast_in_dim | solution.py:464
  153.4 0.0 copy-start.3
  153.4 0.0 copy-start.4
  153.4 0.0 copy-done.2
  153.4 0.8 slice_bitcast_fusion
  154.2 1.6 fusion.2
  155.8 0.0 copy-done.3
  155.8 0.0 copy-done.4
  155.8 1.4 add_bitcast_fusion
  (1 shorter events, 0.0 us)
Async XLA Ops:
  0.6 0.8 copy-start
  0.6 7.2 %copy-start.5 = (f32[128]{0:T(128)S(1)}, f32[128]{0:T(128)}, u32[]{:S(2)}) copy-start(f32[128]{0:T(128)} %param.12) | copy-start | bytes 1540
  0.7 7.2 %copy-start.1 = (bf16[128,2048]{1,0:T(8,128)(2,1)S(1)}, bf16[128,2048]{1,0:T(8,128)(2,1)}, u32[]{:S(2)}) copy-start(bf16[128,2048]{1,0:T(8,128)(2,1)} %param.11) | copy-start | bytes 1572868
  149.5 3.9 %copy-start.2 = (bf16[2,128,2048]{2,1,0:T(8,128)(2,1)S(1)}, bf16[2,128,2048]{2,1,0:T(8,128)(2,1)}, u32[]{:S(2)}) copy-start(bf16[2,128,2048]{2,1,0:T(8,128)(2,1)} %get-tuple-element.13) | copy-start | bytes 3145732
  153.4 2.4 %copy-start.3 = (bf16[384,1024]{1,0:T(8,128)(2,1)S(1)}, bf16[384,1024]{1,0:T(8,128)(2,1)}, u32[]{:S(2)}) copy-start(bf16[384,1024]{1,0:T(8,128)(2,1)} %get-tuple-element.18) | copy-start | bytes 2359300
  153.4 2.4 %copy-start.4 = (bf16[384,1024]{1,0:T(8,128)(2,1)S(1)}, bf16[384,1024]{1,0:T(8,128)(2,1)}, u32[]{:S(2)}) copy-start(bf16[384,1024]{1,0:T(8,128)(2,1)} %get-tuple-element.19) | copy-start | bytes 2359300

commit v3 on v2

--- a/solution.py
+++ b/solution.py
@@ -25,9 +25,9 @@
     n,
     tok_own,
     sca_own,
-    gate_w,
-    up_w,
-    down_w,
+    gate_any,
+    up_any,
+    down_any,
     rows_out,
     kept_gate,
     kept_up,
@@ -56,6 +56,10 @@
     ret_recv,
     dp_send,
     dp_recv,
+    gate_w,
+    up_w,
+    down_w,
+    load_sem,
 ):
     me = lax.axis_index("expert")
     sub = lax.axis_index("sub")
@@ -105,15 +109,22 @@
             {"sub": other},
         )
 
-    def ret_copy(side, dest, slot, kind):
+    def ret_copy(side, dest, slot, kind, piece):
+        rows = pl.ds(piece * (count // 2), count // 2)
         return remote(
-            part.at[dest, kind, sub],
-            z_in.at[slot, kind],
-            ret_send.at[dest, kind],
-            ret_recv.at[slot, kind],
+            part.at[dest, kind, sub, rows],
+            z_in.at[slot, kind, rows],
+            ret_send.at[dest, kind, piece],
+            ret_recv.at[slot, kind, piece],
             toward(side),
         )
 
+    loads = [
+        pltpu.make_async_copy(src, dst, load_sem.at[index])
+        for index, (src, dst) in enumerate(((gate_any, gate_w), (up_any, up_w), (down_any, down_w)))
+    ]
+    for load in loads:
+        load.start()
     barrier = pltpu.get_barrier_semaphore()
 
     @pl.when(has_left)
@@ -141,6 +152,9 @@
             z_copy(kind, 1, 0, me).start()
 
         sib_copy(kind, me, sub).start()
+
+    for load in loads:
+        load.wait()
 
     def arrivals(step):
         for kind in range(2):
@@ -214,16 +228,18 @@
                 @pl.when(valid)
                 def _():
                     part[dest, kind, sub] = add_sibling(dest, kind).astype(jnp.bfloat16)
-
-                    @pl.when(add)
-                    def _():
-                        ret_copy(side, dest, dest, kind).wait_recv()
-                        part[dest, kind, sub] = (
-                            part[dest, kind, sub].astype(jnp.float32)
-                            + z_in[dest, kind].astype(jnp.float32)
-                        ).astype(jnp.bfloat16)
-
-                    ret_copy(side, dest, slot, kind).start()
+                    for piece in range(2):
+                        rows = pl.ds(piece * (count // 2), count // 2)
+
+                        @pl.when(add)
+                        def _():
+                            ret_copy(side, dest, dest, kind, piece).wait_recv()
+                            part[dest, kind, sub, rows] = (
+                                part[dest, kind, sub, rows].astype(jnp.float32)
+                                + z_in[dest, kind, rows].astype(jnp.float32)
+                            ).astype(jnp.bfloat16)
+
+                        ret_copy(side, dest, slot, kind, piece).start()
 
     @pl.loop(0, n)
     def _(time):
@@ -242,7 +258,7 @@
             def _():
                 compute(block)
 
-        @pl.when(time > 0)
+        @pl.when((time > 0) & (time < last))
         def _():
             give_back(step)
 
@@ -277,13 +293,20 @@
                 s = sca[:, :, :, cols].reshape(total, TILE)
                 into[:, there] = dot_f32(hidden_s[...], s, CONTRACT).astype(jnp.bfloat16)
 
-    for kind in range(3):
+    def give_grad(kind):
         weight_grad(kind, (1 - dp) * half, given[kind])
         dp_copy(kind).start()
 
-    @pl.loop(n - 1, 2 * n - 3)
+    give_grad(0)
+
+    @pl.loop(n - 2, 2 * n - 3)
     def _(turn):
         give_back(turn)
+
+        @pl.when(turn == n - 2)
+        def _():
+            give_grad(1)
+            give_grad(2)
 
     for kind in range(3):
         weight_grad(kind, dp * half, kept[kind])
@@ -294,7 +317,8 @@
 
             @pl.when(valid)
             def _():
-                ret_copy(0, me, slot, kind).wait_recv()
+                for piece in range(2):
+                    ret_copy(0, me, slot, kind, piece).wait_recv()
                 rows_out[kind] = (
                     rows_out[kind].astype(jnp.float32) + z_in[slot, kind].astype(jnp.float32)
                 ).astype(jnp.bfloat16)
@@ -307,7 +331,8 @@
 
             @pl.when(block != me)
             def _():
-                ret_copy(0, block, block, kind).wait_send()
+                for piece in range(2):
+                    ret_copy(0, block, block, kind, piece).wait_send()
 
     @pl.loop(0, n - 1)
     def _(step):
@@ -342,7 +367,7 @@
         out_shape=(
             jax.ShapeDtypeStruct((2, count, width), b16), tall, tall, wide, tall, tall, wide,
         ),
-        in_specs=[vmem] * 5,
+        in_specs=[vmem, vmem, hbm, hbm, hbm],
         out_specs=(vmem, vmem, vmem, vmem, hbm, hbm, hbm),
         scratch_shapes=[
             pltpu.VMEM((n, 2, count, width + LANES), b16),
@@ -362,9 +387,13 @@
             dma((2, n)),
             dma((n, 2)),
             dma((n, 2)),
-            dma((n, 2)),
-            dma((n + 1, 2)),
+            dma((n, 2, 2)),
+            dma((n + 1, 2, 2)),
             dma((3,)),
+            dma((3,)),
+            pltpu.VMEM(gate_weight.shape, b16),
+            pltpu.VMEM(up_weight.shape, b16),
+            pltpu.VMEM(down_weight.shape, b16),
             dma((3,)),
         ],
         compiler_params=pltpu.CompilerParams(
@@ -440,8 +469,15 @@
     down_weight,
 ):
     gate_weight, up_weight, down_weight = gate_weight[0], up_weight[0], down_weight[0]
-    copied_expert = hot_experts[copy_slot]
-    expert_id = jnp.where(use_copy == 1, copied_expert[target_device], target_device)
+    slots = jnp.arange(hot_experts.shape[0], dtype=jnp.int32)
+    targets = jnp.arange(copy_slot.shape[0], dtype=jnp.int32)
+    copied_expert = jnp.sum(
+        jnp.where(copy_slot[:, None] == slots[None, :], hot_experts[None, :], 0), axis=1
+    )
+    copied = jnp.sum(
+        jnp.where(target_device[:, None] == targets[None, :], copied_expert[None, :], 0), axis=1
+    )
+    expert_id = jnp.where(use_copy == 1, copied, target_device)
     scaled = (gate_prob[:, None] * cotangent.astype(jnp.float32)).astype(jnp.bfloat16)
     if lax.axis_size("expert") <= 4 and lax.axis_size("dp") == 2 and lax.axis_size("sub") == 2:
         meta = jnp.broadcast_to(

time: 157 us -> 152 us (0.968)
  Pallas kernels: 141 us -> 137 us
    pallas_call x1, Pallas kernels: 141 us -> 137 us  [fused(): pl.pallas_call(functools.partial(fused_kernel, n), out_shape=(jax.ShapeDt...]
    convert_element_type x1, other arithmetic: 3.27 us -> 0.68 us  [on_device(): expert_id.astype(jnp.bfloat16)[:, None]]
where the time goes in v3:
time: 152 us
  Pallas kernels  137 us (90%)
  other arithmetic  12.9 us (8%)
    pallas_call x1, Pallas kernels, fused(): pl.pallas_call(functools.partial(fused_kernel, n), out_shape=(jax.ShapeDt...  137 us
    broadcast_in_dim x1, other arithmetic, on_device(): up_sum[None]  3.92 us

profile of v3, /device:TPU:0, one launch (start us, length us, event | category | flops | bytes accessed | tf_op | source)
XLA Modules:
  0.0 152.0 jit_solution(6798305032868082436)
XLA Ops:
  0.6 0.8 fusion.3
  1.4 0.7 select_reduce_fusion
  2.1 0.7 fusion.4
  2.8 0.1 broadcast_in_dim.51
  2.9 1.9 %pad_maximum_fusion.tok_own = bf16[128,2176]{1,0:T(8,128)(2,1)} fusion(bf16[128,128]{1,0:T(8,128)(2,1)S(1)} %broadcast_in_dim.51, bf16[128,2048]{1,0:T(8,128)(2,1)} %param.10), kind=kLoop, calls=%fused_computation.9 | loop fusion | flops 1114112 | bytes 1114112 | tf_op jit(solution)/shard_map/concatenate | solution.py:486
  4.8 2.0 %fusion.sca_own = bf16[128,2048]{1,0:T(8,128)(2,1)} fusion(bf16[128,2048]{1,0:T(8,128)(2,1)} %param.11, f32[128]{0:T(128)} %param.12), kind=kLoop, calls=%fused_computation.6 | loop fusion | flops 786432 | bytes 1049088 | tf_op jit(solution)/shard_map/convert_element_type | solution.py:481
  6.8 137.4 %shard_map.145 = (bf16[2,128,2048]{2,1,0:T(8,128)(2,1)}, bf16[1024,384]{1,0:T(8,128)(2,1)}, bf16[1024,384]{1,0:T(8,128)(2,1)}, bf16[384,1024]{1,0:T(8,128)(2,1)}...) custom-call(bf16[128,2176]{1,0:T(8,128)(2,1)} %pad_maximum_fusion.tok_own, ...), custom_call_target="tpu_custom_call" | custom-call | flops 14495514624 | bytes 16777216 | tf_op jit(solution)/shard_map/pallas_call | solution.py:365
  144.2 0.0 copy-start.1
  144.2 0.0 copy-start
  144.2 0.0 copy-start.4
  144.3 3.9 %add_bitcast_fusion.1 = (f32[1,1024,384]{2,1,0:T(8,128)}, f32[1,1024,384]{2,1,0:T(8,128)}) fusion(bf16[1024,384]{1,0:T(8,128)(2,1)} %get-tuple-element.17, bf16[1024,384]{1,0:T(8,128)(2,1)} %get-tuple-element.16, bf16[1024,384]{1,0:T(8,128)(2,1)} %get-tuple-element.15, bf16[1024,384]{1,0:T(8,128)(2,1)} %get-tuple-element.14), kind=kLoop, calls=%fused_computation.1 | loop fusion | flops 2359296 | bytes 6291456 | tf_op jit(solution)/shard_map/broadcast_in_dim | solution.py:500
  148.2 0.0 copy-start.2
  148.2 0.0 copy-start.3
  148.2 0.0 copy-done.1
  148.2 0.8 slice_bitcast_fusion
  149.0 0.0 copy-done
  149.0 0.0 copy-done.4
  149.0 1.5 %fusion.2 = (f32[128]{0:T(128)}, bf16[128,2048]{1,0:T(8,128)(2,1)}) fusion(bf16[128,2048]{1,0:T(8,128)(2,1)S(1)} %copy-done, bf16[2,128,2048]{2,1,0:T(8,128)(2,1)S(1)} %copy-done.1, f32[128]{0:T(128)S(1)} %copy-done.4), kind=kLoop, calls=%fused_computation.8 | loop fusion | flops 1572736 | bytes 1573888 | tf_op jit(solution)/shard_map/reduce_sum | solution.py:499
  150.6 0.0 copy-done.2
  150.6 0.0 copy-done.3
  150.6 1.4 add_bitcast_fusion
Async XLA Ops:
  144.2 4.0 %copy-start.1 = (bf16[2,128,2048]{2,1,0:T(8,128)(2,1)S(1)}, bf16[2,128,2048]{2,1,0:T(8,128)(2,1)}, u32[]{:S(2)}) copy-start(bf16[2,128,2048]{2,1,0:T(8,128)(2,1)} %get-tuple-element.13) | copy-start | bytes 3145732
  144.2 4.8 %copy-start = (bf16[128,2048]{1,0:T(8,128)(2,1)S(1)}, bf16[128,2048]{1,0:T(8,128)(2,1)}, u32[]{:S(2)}) copy-start(bf16[128,2048]{1,0:T(8,128)(2,1)} %param.11) | copy-start | bytes 1572868
  144.2 4.8 %copy-start.4 = (f32[128]{0:T(128)S(1)}, f32[128]{0:T(128)}, u32[]{:S(2)}) copy-start(f32[128]{0:T(128)} %param.12) | copy-start | bytes 1540
  148.2 2.4 %copy-start.2 = (bf16[384,1024]{1,0:T(8,128)(2,1)S(1)}, bf16[384,1024]{1,0:T(8,128)(2,1)}, u32[]{:S(2)}) copy-start(bf16[384,1024]{1,0:T(8,128)(2,1)} %get-tuple-element.18) | copy-start | bytes 2359300
  148.2 2.4 %copy-start.3 = (bf16[384,1024]{1,0:T(8,128)(2,1)S(1)}, bf16[384,1024]{1,0:T(8,128)(2,1)}, u32[]{:S(2)}) copy-start(bf16[384,1024]{1,0:T(8,128)(2,1)} %get-tuple-element.19) | copy-start | bytes 2359300
